TPU v7x, 32 devices: a whole 2x2x4 slice. The times are simulated.
32 devices in a mesh: grp: 2 (over y), tok: 4 (over z), feat: 4 (over x, core).
Axes of the slice: x: 2, y: 2, z: 4, core: 2. Of those that a mesh axis runs over, the one named last changes fastest.
Arguments:
- activations: bfloat16 [8192, 14336], P(('grp', 'tok'), 'feat'), parts along dimension 0, may hold values from -6 to 6
- out_grads: bfloat16 [8192, 4096], P(('grp', 'tok'), 'feat'), parts along dimension 0, may hold values from -6 to 6
- input_side_factors: bfloat16 [8, 32, 14336], P('tok', None, 'feat'), may hold values from -0.046875 to 0.046875
- output_factors: bfloat16 [8, 32, 4096], P('tok', None, 'feat'), may hold values from -0.09375 to 0.09375
- query_order: int32 [8], replicated, may hold values from 0 to 7, each once
Outputs:
- scores: float32 [8192, 8], P(('grp', 'tok', 'feat')), parts along dimension 0
There are 2 independent parts, one for each index of `grp`. A program takes and returns all parts, laid end to end along the dimension named above; an argument that names none is the same for every part. Nothing has to cross between parts.
Inputs may be any that keep to these rules, and one draw needn't show every extreme that they name: `query_order`: each query index appears exactly once.
All inputs are finite; a program needn't handle non-finite values.
Results may differ from a plain program's by a relative error of at most 0.0003.
Values may be sent and summed in bfloat16 or wider, within the bound.
A program may use at most 128 MiB of HBM per device.

v0:
```python
import jax
import jax.numpy as jnp
from jax import lax
from jax.sharding import PartitionSpec as P


def project(hidden_activation, grads, right_block, ublock):
    hidden_width = right_block.shape[0] * right_block.shape[1]
    right_matrix = right_block.reshape(hidden_width, right_block.shape[2])
    umat = ublock.reshape(hidden_width, ublock.shape[2])
    contract_dimensions = (((1,), (1,)), ((), ()))
    left_factor = lax.dot_general(
        hidden_activation, right_matrix, contract_dimensions, preferred_element_type=jnp.float32
    )
    right = lax.dot_general(grads, umat, contract_dimensions, preferred_element_type=jnp.float32)
    return (left_factor, right)


def combine(left_factor, right, rank_size):
    rows = left_factor.shape[0]
    count = left_factor.shape[1] // rank_size
    prod = (left_factor * right).reshape(rows, count, rank_size)
    return jnp.sum(prod, axis=2) * rank_size ** (-0.5)


def shards(activations, out_grads, input_side_factors, output_factors, query_order):
    rank_size = input_side_factors.shape[1]
    all_v, all_u = (
        lax.all_gather(input_side_factors, "tok", axis=0, tiled=True),
        lax.all_gather(output_factors, "tok", axis=0, tiled=True),
    )
    left_all, right_all = project(activations, out_grads, all_v, all_u)
    left_own, right_own = (
        lax.psum_scatter(left_all, "feat", scatter_dimension=0, tiled=True),
        lax.psum_scatter(right_all, "feat", scatter_dimension=0, tiled=True),
    )
    raw = combine(left_own, right_own, rank_size)
    return jnp.take(raw, query_order, axis=1)


def solution(mesh):
    return jax.shard_map(
        shards,
        mesh=mesh,
        in_specs=(
            P(("grp", "tok"), "feat"),
            P(("grp", "tok"), "feat"),
            P("tok", None, "feat"),
            P("tok", None, "feat"),
            P(),
        ),
        out_specs=P(("grp", "tok", "feat"), None),
        check_vma=False,
    )
```

profile of v0, /device:TPU:1, one launch (start us, length us, event | category | flops | bytes accessed | tf_op | source)
XLA Modules:
  0.0 95.2 jit_solution(7279757764078991030)
XLA Ops:
  7.4 0.0 copy-start
  7.4 0.0 all-gather.2.cloned.1.call-start
  7.4 0.7 all-gather.2.cloned.1.call-update
  8.1 0.0 reduce-scatter.5.cloned.1.call-start
  8.1 15.5 %all_gather.7 = bf16[8,32,1024]{2,1,0:T(8,128)(2,1)S(1)} all-gather(bf16[2,32,1024]{2,1,0:T(8,128)(2,1)} %param.8), channel_id=1, replica_groups=mesh['grp'=2,'tok'=4,'feat'=4] {'tok'}, dimensions={0}, use_global_device_ids=true | all-gather | bytes 655360 | tf_op jit(solution)/shard_map/all_gather | solution.py:30
  23.6 0.0 copy-done
  23.7 1.7 %fusion.1 = f32[1024,256]{1,0:T(8,128)} fusion(bf16[1024,1024]{1,0:T(8,128)(2,1)S(1)} %copy-done, bf16[256,1024]{1,0:T(8,128)(2,1)S(1)} %bitcast.10), kind=kOutput, calls=%fused_computation.8 | convolution fusion | flops 536870912 | bytes 3670016 | tf_op jit(solution)/shard_map/dot_general | solution.py:15
  25.4 0.0 reduce-scatter.5.cloned.1.call-update
  25.4 0.0 reduce-scatter.3.cloned.1.call-start
  25.5 29.8 %all-gather.2.cloned.1.call-done = bf16[8,32,3584]{2,1,0:T(8,128)(2,1)} async-done(((bf16[2,32,3584]{2,1,0:T(8,128)(2,1)}), bf16[8,32,3584]{2,1,0:T(8,128)(2,1)}) %all-gather.2.cloned.1.call-update) | async-done | bytes 1835024 | tf_op jit(solution)/shard_map/all_gather | solution.py:29
  55.3 0.0 copy-start.1
  55.3 6.6 %fusion = f32[1024,256]{1,0:T(8,128)} fusion(bf16[1024,3584]{1,0:T(8,128)(2,1)} %param.5, bf16[256,3584]{1,0:T(8,128)(2,1)} %bitcast.11), kind=kOutput, calls=%fused_computation.7 | convolution fusion | flops 1879048192 | bytes 10223616 | tf_op jit(solution)/shard_map/dot_general | solution.py:12
  61.9 0.0 reduce-scatter.3.cloned.1.call-update
  62.0 0.0 copy-done.1
  62.0 0.0 reduce-scatter.5.cloned.1.call-done
  62.1 23.2 %reduce-scatter.3.cloned.1.call-done = f32[256,256]{1,0:T(8,128)} async-done(((f32[1024,256]{1,0:T(8,128)}), f32[256,256]{1,0:T(8,128)}) %reduce-scatter.3.cloned.1.call-update) | async-done | bytes 262160 | tf_op jit(solution)/shard_map/reduce_scatter | solution.py:34
  85.3 1.1 %mul.9 = f32[256,256]{1,0:T(8,128)S(1)} multiply(f32[256,256]{1,0:T(8,128)} %reduce-scatter.3.cloned.1.call-done, f32[256,256]{1,0:T(8,128)} %reduce-scatter.5.cloned.1.call-done) | non-fusion elementwise | flops 65536 | bytes 786432 | tf_op jit(solution)/shard_map/mul | solution.py:22
  86.3 0.1 copy.7
  86.5 0.6 gather_fusion
  87.1 0.7 select_bitcast_fusion
  (5 shorter events, 0.1 us)
Async XLA Ops:
  7.4 16.3 %copy-start = (bf16[1024,1024]{1,0:T(8,128)(2,1)S(1)}, bf16[1024,1024]{1,0:T(8,128)(2,1)}, u32[]{:S(2)}) copy-start(bf16[1024,1024]{1,0:T(8,128)(2,1)} %param.6) | copy-start | bytes 6291460
  7.4 47.9 %all-gather.2.cloned.1.call-start = ((), (), s32[]{:S(2)}) async-start(), calls=%async_computation.2 | async-start | bytes 2293760 | tf_op jit(solution)/shard_map/all_gather | solution.py:29
  8.1 54.0 %reduce-scatter.5.cloned.1.call-start = ((), (), s32[]{:S(2)}) async-start(), calls=%async_computation.4 | async-start | bytes 1310720 | tf_op jit(solution)/shard_map/reduce_scatter | solution.py:35
  25.4 59.9 %reduce-scatter.3.cloned.1.call-start = ((), (), s32[]{:S(2)}) async-start(), calls=%async_computation.3 | async-start | bytes 1310720 | tf_op jit(solution)/shard_map/reduce_scatter | solution.py:34
  55.3 6.7 %copy-start.1 = (s32[8]{0:T(128)S(1)}, s32[8]{0:T(128)}, u32[]{:S(2)}) copy-start(s32[8]{0:T(128)} %param.9) | copy-start | bytes 100
Sparse Core Ops, SparseCore 0:
  9.8 45.4 all-gather.1
Sparse Core Ops, SparseCore 1:
  25.5 29.7 reduce-scatter.4
  62.0 23.2 reduce-scatter.2
where the time goes:
time: 96.1 us; the launch traced here: 95.2 us
  waiting for transfers between devices  53.8 us (56%)
  blocking collectives  15.5 us (16%)
  between operations  14.9 us (16%)
  matrix products  8.39 us (9%)
  other arithmetic  1.78 us (2%)
    all_gather x1, waiting for transfers between devices, shards(): lax.all_gather(input_side_factors, 'tok', axis=0, tiled=True)  29.8 us
    reduce_scatter x1, waiting for transfers between devices, shards(): lax.psum_scatter(left_all, 'feat', scatter_dimension=0, tiled=True)  23.2 us
    all_gather x1, blocking collectives, shards(): lax.all_gather(output_factors, 'tok', axis=0, tiled=True)  15.5 us
    dot_general x1, matrix products, project(): lax.dot_general(hidden_activation, right_matrix, contract_dimensions, pre...  6.65 us
  transfers between devices with their start and end apart: 3, of which 2 were waited for; matrix products, arithmetic and copies ran while one was open for 9% of the time, Pallas kernels for 0%

commit v1 on v0

v1 whole, which is shorter than its diff:
```python
import functools

import jax
import jax.numpy as jnp
from jax import lax
from jax.experimental import pallas as pl
from jax.experimental.pallas import tpu as pltpu
from jax.sharding import PartitionSpec as P

MESH = pl.DeviceIdType.MESH
NT = (((1,), (1,)), ((), ()))
PIECES = 3


def segments(left_half, right_half):
    width = (left_half + right_half) // PIECES
    result = []
    for j in range(PIECES):
        lo, hi = j * width, (j + 1) * width
        segs = []
        if lo < left_half:
            segs.append((False, lo, 0, min(hi, left_half) - lo))
        if hi > left_half:
            start = max(lo, left_half)
            segs.append((True, start - left_half, start - lo, hi - start))
        result.append(segs)
    return width, result


def fused(n, rank, a_hbm, g_hbm, v_hbm, u_hbm, order_ref, out_ref,
          a, g, w, part, core_in, pair, pair_in,
          load_a, load_w, z_send, z_recv, y_send, y_recv,
          c_send, c_recv, x_send, x_recv):
    y, z, f = lax.axis_index("grp"), lax.axis_index("tok"), lax.axis_index("feat")
    c, x = lax.rem(f, 2), lax.div(f, 2)
    left_half, right_half = a.shape[1] // 2, g.shape[1] // 2
    width, segs = segments(left_half, right_half)
    rows = w.shape[3]
    chunk = out_ref.shape[1]
    core_mate, x_mate = 2 * x + (1 - c), 2 * (1 - x) + c

    def own_loads(which, h, j):
        made = []
        for i, (is_right, off, at, wide) in enumerate(segs[j]):
            src = u_hbm if is_right else v_hbm
            half = right_half if is_right else left_half
            made.append(pltpu.make_async_copy(
                src.at[:, pl.ds(pl.multiple_of(h * half + off, 128), wide)],
                w.at[z, h, j, :, pl.ds(at, wide)],
                load_w.at[which, j, i]))
        return made

    for which, h in ((0, y), (1, 1 - y)):
        for j in range(PIECES):
            for copy in own_loads(which, h, j):
                copy.start()
    copy_a = pltpu.make_async_copy(a_hbm, a, load_a.at[0])
    copy_g = pltpu.make_async_copy(g_hbm, g, load_a.at[1])
    copy_a.start()
    copy_g.start()

    barrier = pltpu.get_barrier_semaphore()
    pl.semaphore_signal(barrier, inc=1, device_id={"grp": 1 - y}, device_id_type=MESH)
    pl.semaphore_signal(barrier, inc=1, device_id={"feat": core_mate}, device_id_type=MESH)
    pl.semaphore_signal(barrier, inc=1, device_id={"feat": x_mate}, device_id_type=MESH)

    @pl.when(z > 0)
    def _():
        pl.semaphore_signal(barrier, inc=1, device_id={"tok": z - 1}, device_id_type=MESH)

    @pl.when(z < n - 1)
    def _():
        pl.semaphore_signal(barrier, inc=1, device_id={"tok": z + 1}, device_id_type=MESH)

    peers = 3 + jnp.where(z > 0, 1, 0) + jnp.where(z < n - 1, 1, 0)
    pl.semaphore_wait(barrier, peers)

    def source(way, d):
        return z - d if way == 0 else z + d

    def arrives(way, d):
        return z >= d if way == 0 else z < n - d

    def has_next(way):
        return z < n - 1 if way == 0 else z > 0

    def z_copy(way, d, j, s):
        return pltpu.make_async_remote_copy(
            src_ref=w.at[s, y, j], dst_ref=w.at[s, y, j],
            send_sem=z_send.at[way, d - 1, j], recv_sem=z_recv.at[way, d - 1, j],
            device_id={"tok": z + 1 if way == 0 else z - 1}, device_id_type=MESH)

    def y_copy(way, d, j, h):
        s = source(way, d)
        return pltpu.make_async_remote_copy(
            src_ref=w.at[s, h, j], dst_ref=w.at[s, h, j],
            send_sem=y_send.at[way, d - 1, j], recv_sem=y_recv.at[way, d - 1, j],
            device_id={"grp": 1 - y}, device_id_type=MESH)

    def core_copy(b):
        return pltpu.make_async_remote_copy(
            src_ref=part.at[b, 1 - c], dst_ref=core_in.at[b],
            send_sem=c_send.at[b], recv_sem=c_recv.at[b],
            device_id={"feat": core_mate}, device_id_type=MESH)

    def x_copy(b):
        return pltpu.make_async_remote_copy(
            src_ref=pair.at[b], dst_ref=pair_in.at[b],
            send_sem=x_send.at[b], recv_sem=x_recv.at[b],
            device_id={"feat": x_mate}, device_id_type=MESH)

    def add_piece(b, s, h, j, fresh):
        def some_rows(m, carry):
            at_rows = pl.ds(pl.multiple_of(m * chunk, chunk), chunk)
            for is_right, off, at, wide in segs[j]:
                side = g if is_right else a
                half = right_half if is_right else left_half
                columns = pl.ds(pl.multiple_of(h * half + off, 128), wide)
                product = lax.dot_general(
                    side[at_rows, columns], w[s, h, j, :, pl.ds(at, wide)], NT,
                    preferred_element_type=jnp.float32)
                to = (b, lax.rem(m, 2), lax.div(m, 2), slice(None),
                      pl.ds(rows if is_right else 0, rows))
                if fresh and off == 0:
                    part[to] = product
                else:
                    part[to] += product
            return carry

        lax.fori_loop(0, a.shape[0] // chunk, some_rows, 0)

    def across_x(b):
        core_copy(b).wait_recv()
        pair[b] = part[b, c, 1 - x] + core_in[b, 1 - x]
        x_copy(b).start()

    def finish(b, s):
        x_copy(b).wait_recv()
        total = part[b, c, x] + core_in[b, x] + pair_in[b]
        product = total[:, :rows] * total[:, rows:]
        query = s * (rows // rank) + lax.div(
            lax.broadcasted_iota(jnp.int32, (out_ref.shape[0], rows), 1), rank)
        pick = jnp.where(query == order_ref[...], 1.0, 0.0).astype(jnp.float32)
        out_ref[...] += lax.dot_general(
            pick, product, NT, precision=lax.Precision.HIGHEST,
            preferred_element_type=jnp.float32) * (rank ** -0.5)

    def block(way, d):
        return 1 + 2 * (d - 1) + way

    out_ref[...] = jnp.zeros_like(out_ref)
    for j in range(PIECES):
        for copy in own_loads(0, y, j):
            copy.wait()
        for way in (0, 1):
            @pl.when(has_next(way))
            def _():
                z_copy(way, 1, j, z).start()

    def each_way(d, action):
        for way in (0, 1):
            @pl.when(arrives(way, d))
            def _():
                action(way)

    slots = [(d, j) for d in range(1, n) for j in range(PIECES)]

    def other_half(d, j):
        def action(way):
            y_copy(way, d, j, 1 - y).wait_recv()
            add_piece(block(way, d), source(way, d), 1 - y, j, False)
            if j == PIECES - 1:
                core_copy(block(way, d)).start()
        each_way(d, action)

    for k, (d, j) in enumerate(slots):
        def pass_on(way):
            s = source(way, d)
            z_copy(way, d, j, s).wait_recv()
            y_copy(way, d, j, y).start()
            if d < n - 1:
                @pl.when(has_next(way))
                def _():
                    z_copy(way, d + 1, j, s).start()
        each_way(d, pass_on)
        if d == 1:
            if j == 0:
                for jj in range(PIECES):
                    for copy in own_loads(1, 1 - y, jj):
                        copy.wait()
                copy_a.wait()
                copy_g.wait()
            add_piece(0, z, 0, j, True)
            add_piece(0, z, 1, j, False)
            if j == PIECES - 1:
                core_copy(0).start()
        each_way(d, lambda way: add_piece(block(way, d), source(way, d), y, j, True))
        if k >= 1:
            other_half(*slots[k - 1])
        if j == 1:
            if d == 2:
                across_x(0)
            if d >= 2:
                each_way(d - 1, lambda way: across_x(block(way, d - 1)))
        if j == PIECES - 1:
            if d == 2:
                finish(0, z)
            if d >= 3:
                each_way(d - 2, lambda way: finish(block(way, d - 2), source(way, d - 2)))
    other_half(*slots[-1])
    each_way(n - 1, lambda way: across_x(block(way, n - 1)))
    for d in range(max(n - 2, 1), n):
        each_way(d, lambda way: finish(block(way, d), source(way, d)))

    for way in (0, 1):
        for d in range(1, n):
            sends = (arrives(way, d - 1) if d > 1 else z >= 0) & has_next(way)

            @pl.when(sends)
            def _():
                for j in range(PIECES):
                    z_copy(way, d, j, source(way, d - 1)).wait_send()

            @pl.when(arrives(way, d))
            def _():
                for j in range(PIECES):
                    y_copy(way, d, j, y).wait_send()
                core_copy(block(way, d)).wait_send()
                x_copy(block(way, d)).wait_send()
    core_copy(0).wait_send()
    x_copy(0).wait_send()


def fused_shards(n, activations, out_grads, input_side_factors, output_factors, query_order):
    per_block, rank, left = input_side_factors.shape
    right = output_factors.shape[2]
    rows = per_block * rank
    tokens = activations.shape[0]
    chunk = tokens // 4
    total = query_order.shape[0]
    width, segs = segments(left // 2, right // 2)
    most = max(len(s) for s in segs)
    blocks = 2 * n - 1
    dma = pltpu.SemaphoreType.DMA
    f32 = jnp.float32
    return pl.pallas_call(
        functools.partial(fused, n, rank),
        out_shape=jax.ShapeDtypeStruct((total, chunk), f32),
        in_specs=[pl.BlockSpec(memory_space=pl.ANY)] * 4 + [pl.BlockSpec(memory_space=pltpu.VMEM)],
        out_specs=pl.BlockSpec(memory_space=pltpu.VMEM),
        scratch_shapes=[
            pltpu.VMEM((tokens, left), activations.dtype),
            pltpu.VMEM((tokens, right), out_grads.dtype),
            pltpu.VMEM((n, 2, PIECES, rows, width), input_side_factors.dtype),
            pltpu.VMEM((blocks, 2, 2, chunk, 2 * rows), f32),
            pltpu.VMEM((blocks, 2, chunk, 2 * rows), f32),
            pltpu.VMEM((blocks, chunk, 2 * rows), f32),
            pltpu.VMEM((blocks, chunk, 2 * rows), f32),
            dma((2,)),
            dma((2, PIECES, most)),
            dma((2, n - 1, PIECES)),
            dma((2, n - 1, PIECES)),
            dma((2, n - 1, PIECES)),
            dma((2, n - 1, PIECES)),
            dma((blocks,)),
            dma((blocks,)),
            dma((blocks,)),
            dma((blocks,)),
        ],
        compiler_params=pltpu.CompilerParams(
            collective_id=0, has_side_effects=True, vmem_limit_bytes=60 * 2**20),
        cost_estimate=pl.CostEstimate(
            flops=2 * tokens * n * rows * (left + right),
            bytes_accessed=2 * (tokens + rows) * (left + right), transcendentals=0),
    )(
        activations, out_grads,
        input_side_factors.reshape(rows, left), output_factors.reshape(rows, right),
        query_order.reshape(total, 1),
    ).T


def plain_shards(activations, out_grads, input_side_factors, output_factors, query_order):
    rank = input_side_factors.shape[1]
    all_v = lax.all_gather(input_side_factors, "tok", axis=0, tiled=True)
    all_u = lax.all_gather(output_factors, "tok", axis=0, tiled=True)
    sides = []
    for tokens, factors in ((activations, all_v), (out_grads, all_u)):
        matrix = factors.reshape(-1, factors.shape[2])
        partial = lax.dot_general(tokens, matrix, NT, preferred_element_type=jnp.float32)
        sides.append(lax.psum_scatter(partial, "feat", scatter_dimension=0, tiled=True))
    product = (sides[0] * sides[1]).reshape(sides[0].shape[0], -1, rank)
    return jnp.take(jnp.sum(product, axis=2) * rank ** (-0.5), query_order, axis=1)


def solution(mesh):
    n = mesh.shape["tok"]
    small = n <= 4 and mesh.shape["grp"] == 2 and mesh.shape["feat"] == 4
    return jax.shard_map(
        functools.partial(fused_shards, n) if small else plain_shards,
        mesh=mesh,
        in_specs=(
            P(("grp", "tok"), "feat"),
            P(("grp", "tok"), "feat"),
            P("tok", None, "feat"),
            P("tok", None, "feat"),
            P(),
        ),
        out_specs=P(("grp", "tok", "feat"), None),
        check_vma=False,
    )
```

time: 96.1 us -> 51.6 us (0.54)
  waiting for transfers between devices: 53.8 us -> 0 us
  Pallas kernels: 0 us -> 48.8 us
  blocking collectives: 15.5 us -> 0 us
  between operations: 14.9 us -> 0.01 us
  matrix products: 8.39 us -> 0 us
  local copies, waits for them, and re-layouts: 0.7 us -> 2.62 us
  other arithmetic: 1.78 us -> 0 us
    pallas_call x0 -> x1, Pallas kernels: none -> 48.8 us  [fused_shards(): pl.pallas_call(functools.partial(fused, n, rank), out_shape=jax.ShapeDtyp...]
    all_gather x1 -> x0, waiting for transfers between devices: 29.8 us -> none  [shards(): lax.all_gather(input_side_factors, 'tok', axis=0, tiled=True)]
    reduce_scatter x2 -> x0, waiting for transfers between devices: 23.2 us -> none  [the longest x1 23.2 us: shards(): lax.psum_scatter(left_all, 'feat', scatter_dimension=0, tiled=True)]
    all_gather x1 -> x0, blocking collectives: 15.5 us -> none  [shards(): lax.all_gather(output_factors, 'tok', axis=0, tiled=True)]
    dot_general x2 -> x0, matrix products: 8.39 us -> none  [the longest x1 6.65 us: project(): lax.dot_general(hidden_activation, right_matrix, contract_dimensions, pre...]
    reshape x0 -> x1, local copies, waits for them, and re-layouts: none -> 1.32 us  [fused_shards(): query_order.reshape(total, 1)]
    unnamed x4 -> x1, local copies, waits for them, and re-layouts: 0.01 us -> 1.3 us
    mul x2 -> x0, other arithmetic: 1.07 us -> none  [the longest x1 1.06 us: combine(): prod = (left_factor * right).reshape(rows, count, rank_size)]
  transfers between devices with their start and end apart: 3 -> 0, of which waited for: 2 -> 0; matrix products, arithmetic and copies ran while one was open for 9% -> 0% of each run, Pallas kernels for 0% -> 0%
where the time goes in v1:
time: 51.6 us; the launch traced here: 51.4 us
  Pallas kernels  48.8 us (95%)
  local copies, waits for them, and re-layouts  2.62 us (5%)
    pallas_call x1, Pallas kernels, fused_shards(): pl.pallas_call(functools.partial(fused, n, rank), out_shape=jax.ShapeDtyp...  48.8 us
    reshape x1, local copies, waits for them, and re-layouts, fused_shards(): query_order.reshape(total, 1)  1.32 us
    unnamed x1, local copies, waits for them, and re-layouts  1.3 us

profile of v1, /device:TPU:1, one launch (start us, length us, event | category | flops | bytes accessed | tf_op | source)
XLA Modules:
  0.0 51.4 jit_solution(10075681600397784052)
XLA Ops:
  0.0 1.3 %copy.6.order_ref = s32[8,1]{1,0:T(8,128)} copy(s32[8,1]{0,1:T(1,128)} %bitcast.7) | data formatting | bytes 64 | tf_op jit(solution)/shard_map/reshape | solution.py:278
  1.3 48.8 %shard_map.55 = f32[8,256]{1,0:T(8,128)} custom-call(bf16[1024,3584]{1,0:T(8,128)(2,1)} %a_hbm.1, bf16[1024,1024]{1,0:T(8,128)(2,1)} %g_hbm.1, bf16[64,3584]{1,0:T(8,128)(2,1)} %bitcast.4, bf16[64,1024]{1,0:T(8,128)(2,1)} %bitcast.5, s32[8,1]{1,0:T(8,128)} %copy.6.order_ref), custom_call_target="tpu_custom_call" | custom-call | flops 2415919104 | bytes 10027008 | tf_op jit(solution)/shard_map/pallas_call | solution.py:246
  50.1 1.3 %copy.8 = f32[256,8]{0,1:T(8,128)} copy(f32[256,8]{0,1:T(8,128)} %bitcast.6) | data formatting | bytes 16384

commit v2 on v1

--- a/solution.py
+++ b/solution.py
@@ -9,7 +9,7 @@
 
 MESH = pl.DeviceIdType.MESH
 NT = (((1,), (1,)), ((), ()))
-PIECES = 3
+PIECES = 2
 
 
 def segments(left_half, right_half):
@@ -110,24 +110,20 @@
             device_id={"feat": x_mate}, device_id_type=MESH)
 
     def add_piece(b, s, h, j, fresh):
-        def some_rows(m, carry):
-            at_rows = pl.ds(pl.multiple_of(m * chunk, chunk), chunk)
-            for is_right, off, at, wide in segs[j]:
-                side = g if is_right else a
-                half = right_half if is_right else left_half
-                columns = pl.ds(pl.multiple_of(h * half + off, 128), wide)
-                product = lax.dot_general(
-                    side[at_rows, columns], w[s, h, j, :, pl.ds(at, wide)], NT,
-                    preferred_element_type=jnp.float32)
-                to = (b, lax.rem(m, 2), lax.div(m, 2), slice(None),
-                      pl.ds(rows if is_right else 0, rows))
+        for is_right, off, at, wide in segs[j]:
+            side = g if is_right else a
+            half = right_half if is_right else left_half
+            columns = pl.ds(pl.multiple_of(h * half + off, 128), wide)
+            product = lax.dot_general(
+                side[:, columns], w[s, h, j, :, pl.ds(at, wide)], NT,
+                preferred_element_type=jnp.float32)
+            for m in range(4):
+                to = (b, m % 2, m // 2, slice(None), pl.ds(rows if is_right else 0, rows))
+                some = product[m * chunk:(m + 1) * chunk]
                 if fresh and off == 0:
-                    part[to] = product
+                    part[to] = some
                 else:
-                    part[to] += product
-            return carry
-
-        lax.fori_loop(0, a.shape[0] // chunk, some_rows, 0)
+                    part[to] += some
 
     def across_x(b):
         core_copy(b).wait_recv()
@@ -140,7 +136,11 @@
         product = total[:, :rows] * total[:, rows:]
         query = s * (rows // rank) + lax.div(
             lax.broadcasted_iota(jnp.int32, (out_ref.shape[0], rows), 1), rank)
-        pick = jnp.where(query == order_ref[...], 1.0, 0.0).astype(jnp.float32)
+        column = lax.broadcasted_iota(jnp.int32, query.shape, 0)
+        wanted = jnp.zeros_like(query)
+        for k in range(out_ref.shape[0]):
+            wanted = jnp.where(column == k, order_ref[k], wanted)
+        pick = jnp.where(query == wanted, 1.0, 0.0).astype(jnp.float32)
         out_ref[...] += lax.dot_general(
             pick, product, NT, precision=lax.Precision.HIGHEST,
             preferred_element_type=jnp.float32) * (rank ** -0.5)
@@ -197,7 +197,7 @@
         each_way(d, lambda way: add_piece(block(way, d), source(way, d), y, j, True))
         if k >= 1:
             other_half(*slots[k - 1])
-        if j == 1:
+        if j == min(1, PIECES - 1):
             if d == 2:
                 across_x(0)
             if d >= 2:
@@ -246,7 +246,7 @@
     return pl.pallas_call(
         functools.partial(fused, n, rank),
         out_shape=jax.ShapeDtypeStruct((total, chunk), f32),
-        in_specs=[pl.BlockSpec(memory_space=pl.ANY)] * 4 + [pl.BlockSpec(memory_space=pltpu.VMEM)],
+        in_specs=[pl.BlockSpec(memory_space=pl.ANY)] * 4 + [pl.BlockSpec(memory_space=pltpu.SMEM)],
         out_specs=pl.BlockSpec(memory_space=pltpu.VMEM),
         scratch_shapes=[
             pltpu.VMEM((tokens, left), activations.dtype),
@@ -275,7 +275,7 @@
     )(
         activations, out_grads,
         input_side_factors.reshape(rows, left), output_factors.reshape(rows, right),
-        query_order.reshape(total, 1),
+        query_order,
     ).T
 
 

time: 51.6 us -> 42.2 us (0.82)
  Pallas kernels: 48.8 us -> 40.7 us
  local copies, waits for them, and re-layouts: 2.62 us -> 1.3 us
    pallas_call x1, Pallas kernels: 48.8 us -> 40.7 us  [fused_shards(): pl.pallas_call(functools.partial(fused, n, rank), out_shape=jax.ShapeDtyp...]
    reshape x1 -> x0, local copies, waits for them, and re-layouts: 1.32 us -> none  [fused_shards(): query_order.reshape(total, 1)]
where the time goes in v2:
time: 42.2 us; the launch traced here: 42 us
  Pallas kernels  40.7 us (96%)
  local copies, waits for them, and re-layouts  1.3 us (3%)
    pallas_call x1, Pallas kernels, fused_shards(): pl.pallas_call(functools.partial(fused, n, rank), out_shape=jax.ShapeDtyp...  40.7 us
    unnamed x1, local copies, waits for them, and re-layouts  1.3 us

profile of v2, /device:TPU:1, one launch (start us, length us, event | category | flops | bytes accessed | tf_op | source)
XLA Modules:
  0.0 42.0 jit_solution(2714140091442228864)
XLA Ops:
  0.0 40.7 %shard_map.55 = f32[8,256]{1,0:T(8,128)} custom-call(bf16[1024,3584]{1,0:T(8,128)(2,1)} %a_hbm.1, bf16[1024,1024]{1,0:T(8,128)(2,1)} %g_hbm.1, bf16[64,3584]{1,0:T(8,128)(2,1)} %bitcast.3, bf16[64,1024]{1,0:T(8,128)(2,1)} %bitcast.4, s32[8]{0:T(128)} %order_ref.1), custom_call_target="tpu_custom_call" | custom-call | flops 2415919104 | bytes 10027008 | tf_op jit(solution)/shard_map/pallas_call | solution.py:246
  40.7 1.3 %copy.7 = f32[256,8]{0,1:T(8,128)} copy(f32[256,8]{0,1:T(8,128)} %bitcast.5) | data formatting | bytes 16384

commit v3 on v2

--- a/solution.py
+++ b/solution.py
@@ -9,7 +9,7 @@
 
 MESH = pl.DeviceIdType.MESH
 NT = (((1,), (1,)), ((), ()))
-PIECES = 2
+PIECES = 3
 
 
 def segments(left_half, right_half):
@@ -30,12 +30,12 @@
 def fused(n, rank, a_hbm, g_hbm, v_hbm, u_hbm, order_ref, out_ref,
           a, g, w, part, core_in, pair, pair_in,
           load_a, load_w, z_send, z_recv, y_send, y_recv,
-          c_send, c_recv, x_send, x_recv):
+          c_send, c_recv, x_send, x_recv, e_send, e_recv):
     y, z, f = lax.axis_index("grp"), lax.axis_index("tok"), lax.axis_index("feat")
     c, x = lax.rem(f, 2), lax.div(f, 2)
     left_half, right_half = a.shape[1] // 2, g.shape[1] // 2
     width, segs = segments(left_half, right_half)
-    rows = w.shape[3]
+    rows, last = w.shape[3], PIECES - 1
     chunk = out_ref.shape[1]
     core_mate, x_mate = 2 * x + (1 - c), 2 * (1 - x) + c
 
@@ -89,6 +89,21 @@
             src_ref=w.at[s, y, j], dst_ref=w.at[s, y, j],
             send_sem=z_send.at[way, d - 1, j], recv_sem=z_recv.at[way, d - 1, j],
             device_id={"tok": z + 1 if way == 0 else z - 1}, device_id_type=MESH)
+
+    def from_end(way, d):
+        return z == d if way == 0 else z == n - 1 - d
+
+    def extra_copy(way, d, s):
+        return pltpu.make_async_remote_copy(
+            src_ref=w.at[s, 1 - y, last], dst_ref=w.at[s, 1 - y, last],
+            send_sem=e_send.at[way, d - 1], recv_sem=e_recv.at[way, d - 1],
+            device_id={"tok": z + 1 if way == 0 else z - 1}, device_id_type=MESH)
+
+    def unless_extra(way, d, j, action):
+        if j == last:
+            pl.when(jnp.logical_not(from_end(way, d)))(action)
+        else:
+            action()
 
     def y_copy(way, d, j, h):
         s = source(way, d)
@@ -156,6 +171,13 @@
             @pl.when(has_next(way))
             def _():
                 z_copy(way, 1, j, z).start()
+    for j in range(PIECES):
+        for copy in own_loads(1, 1 - y, j):
+            copy.wait()
+    for way in (0, 1):
+        @pl.when(from_end(way, 0))
+        def _():
+            extra_copy(way, 1, z).start()
 
     def each_way(d, action):
         for way in (0, 1):
@@ -167,7 +189,7 @@
 
     def other_half(d, j):
         def action(way):
-            y_copy(way, d, j, 1 - y).wait_recv()
+            unless_extra(way, d, j, lambda: y_copy(way, d, j, 1 - y).wait_recv())
             add_piece(block(way, d), source(way, d), 1 - y, j, False)
             if j == PIECES - 1:
                 core_copy(block(way, d)).start()
@@ -177,7 +199,7 @@
         def pass_on(way):
             s = source(way, d)
             z_copy(way, d, j, s).wait_recv()
-            y_copy(way, d, j, y).start()
+            unless_extra(way, d, j, lambda: y_copy(way, d, j, y).start())
             if d < n - 1:
                 @pl.when(has_next(way))
                 def _():
@@ -185,9 +207,6 @@
         each_way(d, pass_on)
         if d == 1:
             if j == 0:
-                for jj in range(PIECES):
-                    for copy in own_loads(1, 1 - y, jj):
-                        copy.wait()
                 copy_a.wait()
                 copy_g.wait()
             add_piece(0, z, 0, j, True)
@@ -197,6 +216,13 @@
         each_way(d, lambda way: add_piece(block(way, d), source(way, d), y, j, True))
         if k >= 1:
             other_half(*slots[k - 1])
+        if j == last:
+            for way in (0, 1):
+                @pl.when(from_end(way, d))
+                def _():
+                    extra_copy(way, d, source(way, d)).wait_recv()
+                    if d < n - 1:
+                        extra_copy(way, d + 1, source(way, d)).start()
         if j == min(1, PIECES - 1):
             if d == 2:
                 across_x(0)
@@ -214,6 +240,10 @@
 
     for way in (0, 1):
         for d in range(1, n):
+            @pl.when(from_end(way, d - 1))
+            def _():
+                extra_copy(way, d, source(way, d - 1)).wait_send()
+
             sends = (arrives(way, d - 1) if d > 1 else z >= 0) & has_next(way)
 
             @pl.when(sends)
@@ -224,7 +254,7 @@
             @pl.when(arrives(way, d))
             def _():
                 for j in range(PIECES):
-                    y_copy(way, d, j, y).wait_send()
+                    unless_extra(way, d, j, lambda: y_copy(way, d, j, y).wait_send())
                 core_copy(block(way, d)).wait_send()
                 x_copy(block(way, d)).wait_send()
     core_copy(0).wait_send()
@@ -266,6 +296,8 @@
             dma((blocks,)),
             dma((blocks,)),
             dma((blocks,)),
+            dma((2, n - 1)),
+            dma((2, n - 1)),
         ],
         compiler_params=pltpu.CompilerParams(
             collective_id=0, has_side_effects=True, vmem_limit_bytes=60 * 2**20),
@@ -294,7 +326,7 @@
 
 def solution(mesh):
     n = mesh.shape["tok"]
-    small = n <= 4 and mesh.shape["grp"] == 2 and mesh.shape["feat"] == 4
+    small = 2 <= n <= 4 and mesh.shape["grp"] == 2 and mesh.shape["feat"] == 4
     return jax.shard_map(
         functools.partial(fused_shards, n) if small else plain_shards,
         mesh=mesh,

time: 42.2 us -> 40.1 us (0.950)
  Pallas kernels: 40.7 us -> 38.5 us
    pallas_call x1, Pallas kernels: 40.7 us -> 38.5 us  [fused_shards(): pl.pallas_call(functools.partial(fused, n, rank), out_shape=jax.ShapeDtyp...]
where the time goes in v3:
time: 40.1 us; the launch traced here: 39.9 us
  Pallas kernels  38.5 us (96%)
  local copies, waits for them, and re-layouts  1.3 us (3%)
    pallas_call x1, Pallas kernels, fused_shards(): pl.pallas_call(functools.partial(fused, n, rank), out_shape=jax.ShapeDtyp...  38.5 us
    unnamed x1, local copies, waits for them, and re-layouts  1.3 us

profile of v3, /device:TPU:1, one launch (start us, length us, event | category | flops | bytes accessed | tf_op | source)
XLA Modules:
  0.0 39.9 jit_solution(10227090720624008161)
XLA Ops:
  0.0 38.5 %shard_map.55 = f32[8,256]{1,0:T(8,128)} custom-call(bf16[1024,3584]{1,0:T(8,128)(2,1)} %a_hbm.1, bf16[1024,1024]{1,0:T(8,128)(2,1)} %g_hbm.1, bf16[64,3584]{1,0:T(8,128)(2,1)} %bitcast.3, bf16[64,1024]{1,0:T(8,128)(2,1)} %bitcast.4, s32[8]{0:T(128)} %order_ref.1), custom_call_target="tpu_custom_call" | custom-call | flops 2415919104 | bytes 10027008 | tf_op jit(solution)/shard_map/pallas_call | solution.py:276
  38.6 1.3 %copy.7 = f32[256,8]{0,1:T(8,128)} copy(f32[256,8]{0,1:T(8,128)} %bitcast.5) | data formatting | bytes 16384

commit v4 on v3

--- a/solution.py
+++ b/solution.py
@@ -39,6 +39,19 @@
     chunk = out_ref.shape[1]
     core_mate, x_mate = 2 * x + (1 - c), 2 * (1 - x) + c
 
+    barrier = pltpu.get_barrier_semaphore()
+    pl.semaphore_signal(barrier, inc=1, device_id={"grp": 1 - y}, device_id_type=MESH)
+    pl.semaphore_signal(barrier, inc=1, device_id={"feat": core_mate}, device_id_type=MESH)
+    pl.semaphore_signal(barrier, inc=1, device_id={"feat": x_mate}, device_id_type=MESH)
+
+    @pl.when(z > 0)
+    def _():
+        pl.semaphore_signal(barrier, inc=1, device_id={"tok": z - 1}, device_id_type=MESH)
+
+    @pl.when(z < n - 1)
+    def _():
+        pl.semaphore_signal(barrier, inc=1, device_id={"tok": z + 1}, device_id_type=MESH)
+
     def own_loads(which, h, j):
         made = []
         for i, (is_right, off, at, wide) in enumerate(segs[j]):
@@ -58,19 +71,6 @@
     copy_g = pltpu.make_async_copy(g_hbm, g, load_a.at[1])
     copy_a.start()
     copy_g.start()
-
-    barrier = pltpu.get_barrier_semaphore()
-    pl.semaphore_signal(barrier, inc=1, device_id={"grp": 1 - y}, device_id_type=MESH)
-    pl.semaphore_signal(barrier, inc=1, device_id={"feat": core_mate}, device_id_type=MESH)
-    pl.semaphore_signal(barrier, inc=1, device_id={"feat": x_mate}, device_id_type=MESH)
-
-    @pl.when(z > 0)
-    def _():
-        pl.semaphore_signal(barrier, inc=1, device_id={"tok": z - 1}, device_id_type=MESH)
-
-    @pl.when(z < n - 1)
-    def _():
-        pl.semaphore_signal(barrier, inc=1, device_id={"tok": z + 1}, device_id_type=MESH)
 
     peers = 3 + jnp.where(z > 0, 1, 0) + jnp.where(z < n - 1, 1, 0)
     pl.semaphore_wait(barrier, peers)
@@ -199,11 +199,11 @@
         def pass_on(way):
             s = source(way, d)
             z_copy(way, d, j, s).wait_recv()
-            unless_extra(way, d, j, lambda: y_copy(way, d, j, y).start())
             if d < n - 1:
                 @pl.when(has_next(way))
                 def _():
                     z_copy(way, d + 1, j, s).start()
+            unless_extra(way, d, j, lambda: y_copy(way, d, j, y).start())
         each_way(d, pass_on)
         if d == 1:
             if j == 0:

time: 40.1 us -> 39.9 us (level)
  no operation moved by 1% of the time
where the time goes in v4:
time: 39.9 us; the launch traced here: 39.7 us
  Pallas kernels  38.4 us (96%)
  local copies, waits for them, and re-layouts  1.3 us (3%)
    pallas_call x1, Pallas kernels, fused_shards(): pl.pallas_call(functools.partial(fused, n, rank), out_shape=jax.ShapeDtyp...  38.4 us
    unnamed x1, local copies, waits for them, and re-layouts  1.3 us

profile of v4, /device:TPU:1, one launch (start us, length us, event | category | flops | bytes accessed | tf_op | source)
XLA Modules:
  0.0 39.7 jit_solution(14119862058344662050)
XLA Ops:
  0.0 38.4 %shard_map.55 = f32[8,256]{1,0:T(8,128)} custom-call(bf16[1024,3584]{1,0:T(8,128)(2,1)} %a_hbm.1, bf16[1024,1024]{1,0:T(8,128)(2,1)} %g_hbm.1, bf16[64,3584]{1,0:T(8,128)(2,1)} %bitcast.3, bf16[64,1024]{1,0:T(8,128)(2,1)} %bitcast.4, s32[8]{0:T(128)} %order_ref.1), custom_call_target="tpu_custom_call" | custom-call | flops 2415919104 | bytes 10027008 | tf_op jit(solution)/shard_map/pallas_call | solution.py:276
  38.4 1.3 %copy.7 = f32[256,8]{0,1:T(8,128)} copy(f32[256,8]{0,1:T(8,128)} %bitcast.5) | data formatting | bytes 16384
